TPU v7x, 32 devices: a whole 2x2x4 slice. The times are simulated.
32 devices in a mesh: rep: 8 (over z, y), tp: 4 (over x, core).
Axes of the slice: x: 2, y: 2, z: 4, core: 2. Of those that a mesh axis runs over, the one named last changes fastest.
Arguments:
- gradients: bfloat16 [8, 1024, 1024], P('rep', None, 'tp'), may hold values from -6 to 6
- feedback: float32 [8, 1024, 1024], P('rep', None, 'tp'), may hold values from -4 to 4
- warm_factor: float32 [1024, 32], P('tp'), may hold values from -0.1875 to 0.1875
- momentum: float32 [1024, 1024], P('rep', 'tp'), may hold values from -3 to 3
- master_owned: float32 [1024, 1024], P('rep', 'tp'), may hold values from -4 to 4
- vector_grads: float32 [8, 2560], P('rep'), may hold values from -6 to 6
- vector_params: float32 [2560], replicated, may hold values from 0.5 to 1.5
- vector_momentum: float32 [2560], replicated, may hold values from -3 to 3
Outputs:
- new_feedback: float32 [8, 1024, 1024], P('rep', None, 'tp')
- new_momentum: float32 [1024, 1024], P('rep', 'tp')
- new_master: float32 [1024, 1024], P('rep', 'tp')
- weight: bfloat16 [1024, 1024], P(None, 'tp')
- new_vector_params: float32 [2560], replicated
- new_vector_momentum: float32 [2560], replicated
All inputs are finite; a program needn't handle non-finite values.
Results may differ from a plain program's by a relative error of at most 0.0049.
Values may be sent and summed in bfloat16 or wider, within the bound.
A program may use at most 64 MiB of HBM per device.

v0:
```python
import jax
import jax.numpy as jnp
from jax import lax
from jax.sharding import PartitionSpec as P

PRECISE = lax.Precision.HIGHEST
MOMENTUM_RATE = 0.9
LEARN_RATE = 0.5


def left_factor(combined, factor):
    partial_terms = jnp.dot(combined, factor, precision=PRECISE)
    return lax.psum(partial_terms, ("rep", "tp"))


def orthonormal(left):
    gram = jnp.dot(left.T, left, precision=PRECISE)
    lower = jnp.linalg.cholesky(gram)
    return jax.scipy.linalg.solve_triangular(lower, left.T, lower=True).T


def right_terms(combined, ortho):
    return lax.dot_general(combined, ortho, (((0,), (0,)), ((), ())), precision=PRECISE)


def shards(
    gradients,
    feedback,
    warm_factor,
    momentum,
    master_owned,
    vector_grads,
    vector_params,
    vector_momentum,
):
    replicas = lax.axis_size("rep")
    combined = gradients[0].astype(jnp.float32) + feedback[0]
    vector_sum = lax.psum(vector_grads[0], "rep")
    left_one = left_factor(combined, warm_factor)
    ortho_one = orthonormal(left_one)
    right_one = lax.psum(right_terms(combined, ortho_one), "rep")
    left_two = left_factor(combined, right_one)
    ortho_two = orthonormal(left_two)
    right_two = lax.psum(right_terms(combined, ortho_two), "rep")
    approx = jnp.dot(ortho_two, right_two.T, precision=PRECISE) / replicas
    new_feedback = (combined - approx)[None]
    owned_rows = momentum.shape[0]
    row_start = lax.axis_index("rep") * owned_rows
    owned_approx = lax.dynamic_slice_in_dim(approx, row_start, owned_rows, 0)
    new_momentum = MOMENTUM_RATE * momentum + owned_approx
    new_master = master_owned - LEARN_RATE * new_momentum
    weight = lax.all_gather(new_master.astype(jnp.bfloat16), "rep", axis=0, tiled=True)
    new_vector_momentum = MOMENTUM_RATE * vector_momentum + vector_sum / replicas
    new_vector_params = vector_params - LEARN_RATE * new_vector_momentum
    return (new_feedback, new_momentum, new_master, weight, new_vector_params, new_vector_momentum)


def solution(mesh):
    return jax.shard_map(
        shards,
        mesh=mesh,
        in_specs=(
            P("rep", None, "tp"),
            P("rep", None, "tp"),
            P("tp", None),
            P("rep", "tp"),
            P("rep", "tp"),
            P("rep", None),
            P(),
            P(),
        ),
        out_specs=(P("rep", None, "tp"), P("rep", "tp"), P("rep", "tp"), P(None, "tp"), P(), P()),
        check_vma=False,
    )
```

profile of v0, /device:TPU:0, one launch (start us, length us, event | category | flops | bytes accessed | tf_op | source)
XLA Modules:
  0.0 399.2 jit_solution(9243937694480524052)
XLA Ops:
  7.2 0.0 copy-start
  7.2 0.0 copy-start.1
  7.2 0.0 all-reduce.4.cloned.1.call-start
  7.2 0.7 copy-done
  7.9 3.1 fusion.6
  11.1 0.0 copy-start.2
  11.1 0.0 all-reduce.4.cloned.1.call-update
  11.1 0.0 all-reduce.6.cloned.1.call-start
  11.1 128.1 %all-reduce.4.cloned.1.call-done = f32[1024,32]{0,1:T(8,128)} async-done(((f32[1024,32]{0,1:T(8,128)}), f32[1024,32]{0,1:T(8,128)}) %all-reduce.4.cloned.1.call-update) | async-done | bytes 131088 | tf_op jit(solution)/shard_map/psum | solution.py:13
  139.3 1.2 fusion.22
  140.5 0.1 copy.14
  140.6 2.9 cholesky.44
  143.5 0.6 compare_reduce_fusion.1
  144.2 0.7 fusion.13
  144.8 2.4 custom-call.6
  147.3 1.2 fusion.11
  148.5 0.0 copy-done.1
  148.5 0.0 copy-done.2
  148.5 1.8 fusion.4
  150.4 37.3 %psum.36 = f32[256,32]{1,0:T(8,128)S(1)} all-reduce(f32[256,32]{1,0:T(8,128)S(1)} %fusion.4), channel_id=1, replica_groups=mesh['rep'=8,'tp'=4] {'rep'}, use_global_device_ids=true, to_apply=%region_3.0 | all-reduce | flops 8192 | bytes 65536 | tf_op jit(solution)/shard_map/psum | solution.py:41
  187.7 1.8 fusion.2
  189.5 0.0 all-reduce.6.cloned.1.call-update
  189.5 0.0 copy-start.8
  189.5 0.7 copy-done.8
  190.3 118.2 %all-reduce.6.cloned.1.call-done = f32[1024,32]{0,1:T(8,128)} async-done(((f32[1024,32]{0,1:T(8,128)}), f32[1024,32]{0,1:T(8,128)}) %all-reduce.6.cloned.1.call-update) | async-done | bytes 131088 | tf_op jit(solution)/shard_map/psum | solution.py:13
  308.5 1.2 fusion.23
  309.7 0.0 copy-start.3
  309.7 0.1 copy.15
  309.8 2.9 cholesky.55
  312.8 0.6 compare_reduce_fusion
  313.4 0.7 fusion.14
  314.1 2.4 custom-call.7
  316.5 0.0 copy-done.3
  316.5 0.3 fusion.9
  316.8 1.8 fusion
  318.6 37.9 %all-reduce = (f32[256,32]{1,0:T(8,128)S(1)}, f32[2560]{0:T(1024)S(1)}) all-reduce(f32[256,32]{1,0:T(8,128)S(1)} %fusion, f32[2560]{0:T(1024)S(1)} %reduce.4), channel_id=1, replica_groups=mesh['rep'=8,'tp'=4] {'rep'}, use_global_device_ids=true, to_apply=%region_5.8 | all-reduce | flops 10752 | bytes 86016 | tf_op jit(solution)/shard_map/psum | solution.py:44
  356.6 1.0 convolution_multiply_fusion
  357.6 0.0 copy-start.4
  357.6 0.0 copy-start.5
  357.6 1.2 fusion.8
  358.8 0.0 copy-done.4
  358.8 0.0 copy-done.5
  358.8 0.7 fusion.21
  359.5 31.4 %all_gather.3 = bf16[1024,256]{1,0:T(8,128)(2,1)S(1)} all-gather(bf16[128,256]{1,0:T(8,128)(2,1)S(1)} %get-tuple-element.12), channel_id=1, replica_groups=mesh['rep'=8,'tp'=4] {'rep'}, dimensions={0}, use_global_device_ids=true | all-gather | bytes 589824 | tf_op jit(solution)/shard_map/all_gather | solution.py:52
  390.9 0.0 copy-done.6
  390.9 0.0 copy-done.7
  390.9 0.6 multiply_subtract_fusion.1
  391.6 0.8 copy.19
  (7 shorter events, 0.1 us)
Async XLA Ops:
  7.2 0.8 copy-start
  7.2 141.3 %copy-start.1 = (f32[1,1024,256]{2,1,0:T(8,128)S(1)}, f32[1,1024,256]{2,1,0:T(8,128)}, u32[]{:S(2)}) copy-start(f32[1,1024,256]{2,1,0:T(8,128)} %param.12) | copy-start | bytes 3145732
  7.2 132.1 %all-reduce.4.cloned.1.call-start = ((), (), s32[]{:S(2)}) async-start(), calls=%async_computation | async-start | bytes 262144 | tf_op jit(solution)/shard_map/psum | solution.py:13
  11.1 137.5 %copy-start.2 = (bf16[1,1024,256]{2,1,0:T(8,128)(2,1)S(1)}, bf16[1,1024,256]{2,1,0:T(8,128)(2,1)}, u32[]{:S(2)}) copy-start(bf16[1,1024,256]{2,1,0:T(8,128)(2,1)} %param.11) | copy-start | bytes 1572868
  11.1 297.4 %all-reduce.6.cloned.1.call-start = ((), (), s32[]{:S(2)}) async-start(), calls=%async_computation.1 | async-start | bytes 262144 | tf_op jit(solution)/shard_map/psum | solution.py:13
  189.5 0.7 copy-start.8
  309.7 6.8 %copy-start.3 = (f32[1024,32]{0,1:T(8,128)S(1)}, f32[1024,32]{0,1:T(8,128)}, u32[]{:S(2)}) copy-start(f32[1024,32]{0,1:T(8,128)} %all-reduce.6.cloned.1.call-done) | copy-start | bytes 393220
  357.6 1.2 copy-start.4
  357.6 1.2 copy-start.5
  359.5 31.4 %copy-start.6 = (f32[2560]{0:T(1024)S(1)}, f32[2560]{0:T(1024)}, u32[]{:S(2)}) copy-start(f32[2560]{0:T(1024)} %param.17) | copy-start | bytes 30724
  359.5 31.4 %copy-start.7 = (f32[2560]{0:T(1024)S(1)}, f32[2560]{0:T(1024)}, u32[]{:S(2)}) copy-start(f32[2560]{0:T(1024)} %param.18) | copy-start | bytes 30724
Sparse Core Ops, SparseCore 0:
  14.1 125.0 all-reduce.3
  189.6 118.7 all-reduce.5
where the time goes:
time: 400 us; the launch traced here: 399 us
  waiting for transfers between devices  246 us (62%)
  blocking collectives  107 us (27%)
  other arithmetic  15.9 us (4%)
  between operations  14.2 us (4%)
  matrix products  13.6 us (3%)
    psum x2, waiting for transfers between devices, left_factor(): return lax.psum(partial_terms, ('rep', 'tp'))  246 us
    psum x1, blocking collectives, shards(): right_two = lax.psum(right_terms(combined, ortho_two), 'rep')  37.9 us
    psum x1, blocking collectives, shards(): right_one = lax.psum(right_terms(combined, ortho_one), 'rep')  37.3 us
    all_gather x1, blocking collectives, shards(): lax.all_gather(new_master.astype(jnp.bfloat16), 'rep', axis=0, tiled=True)  31.4 us
  transfers between devices with their start and end apart: 2, of which 2 were waited for; matrix products, arithmetic and copies ran while one was open for 0% of the time, Pallas kernels for 0%

commit v1 on v0

--- a/solution.py
+++ b/solution.py
@@ -1,6 +1,10 @@
+import functools
+
 import jax
 import jax.numpy as jnp
 from jax import lax
+from jax.experimental import pallas as pl
+from jax.experimental.pallas import tpu as pltpu
 from jax.sharding import PartitionSpec as P
 
 PRECISE = lax.Precision.HIGHEST
@@ -55,9 +59,362 @@
     return (new_feedback, new_momentum, new_master, weight, new_vector_params, new_vector_momentum)
 
 
+LANES = 128
+SUBLANES = 8
+NT = (((1,), (1,)), ((), ()))
+NN = (((1,), (0,)), ((), ()))
+TN = (((0,), (0,)), ((), ()))
+
+
+def dot16(a, b, dims):
+    return lax.dot_general(a, b, dims, preferred_element_type=jnp.float32)
+
+
+def split(x):
+    high = x.astype(jnp.bfloat16)
+    return high, (x - high.astype(jnp.float32)).astype(jnp.bfloat16)
+
+
+def times_parts(a, high, low, dims):
+    a_high, a_low = split(a)
+    rank = a.shape[0]
+    both = dot16(jnp.concatenate([a_high, a_low], axis=0), high, dims)
+    return both[:rank] + both[rank:] + dot16(a_high, low, dims)
+
+
+def gram_of(left_t):
+    rank = left_t.shape[0]
+    high, rest = left_t.astype(jnp.bfloat16), None
+    rest = left_t - high.astype(jnp.float32)
+    middle = rest.astype(jnp.bfloat16)
+    low = (rest - middle.astype(jnp.float32)).astype(jnp.bfloat16)
+    parts = jnp.concatenate([high, middle, low], axis=0)
+    grid = dot16(parts, parts, NT)
+    rows = grid[:rank] + grid[rank : 2 * rank] + grid[2 * rank :]
+    return rows[:, :rank] + rows[:, rank : 2 * rank] + rows[:, 2 * rank :]
+
+
+def inverse_lower(gram):
+    rank = gram.shape[0]
+    row_id = lax.broadcasted_iota(jnp.int32, (rank, 2 * rank), 0)
+    lane_id = lax.broadcasted_iota(jnp.int32, (rank, 2 * rank), 1)
+    unit = (lane_id == row_id + rank).astype(jnp.float32)
+    work = jnp.concatenate([gram, unit[:, rank:]], axis=1)
+    for j in range(rank):
+        scale = lax.rsqrt(work[j : j + 1, j : j + 1])
+        row = work[j : j + 1, :] * scale
+        column = work[:, j : j + 1] * scale
+        work = jnp.where(row_id < j, work, jnp.where(row_id == j, row, work - column * row))
+    return work[:, rank:]
+
+
+def step_kernel(
+    reps,
+    tps,
+    grad_ref,
+    feed_ref,
+    warm_ref,
+    mom_ref,
+    master_ref,
+    vgrad_ref,
+    vpar_ref,
+    vmom_ref,
+    new_feed_ref,
+    new_mom_ref,
+    new_master_ref,
+    weight_ref,
+    new_vpar_ref,
+    new_vmom_ref,
+    pair_send,
+    pair_recv,
+    line_send,
+    line_recv,
+    base_all,
+    tp_send,
+    tp_recv,
+    left_all,
+    piece_send,
+    piece_recv,
+    right_all,
+    vec_all,
+    ortho_parts,
+    pair_ss,
+    pair_rs,
+    line_ss,
+    line_rs,
+    base_ss,
+    base_rs,
+    fwd_ss,
+    fwd_rs,
+    tp_ss,
+    tp_rs,
+    left_ss,
+    left_rs,
+    piece_ss,
+    piece_rs,
+    right_ss,
+    right_rs,
+    vec_ss,
+    vec_rs,
+):
+    me = lax.axis_index("rep")
+    col = lax.axis_index("tp")
+    lines = reps // 2
+    far, near = me // 2, me % 2
+    partner = far * 2 + (1 - near)
+    rows, cols = mom_ref.shape
+    rank = warm_ref.shape[1]
+    half = rank // SUBLANES
+
+    def rep_peer(k):
+        return lax.rem(me + k, reps)
+
+    def tp_peer(k):
+        return lax.rem(col + k, tps)
+
+    def line_at(d):
+        return lax.rem(far + d, lines)
+
+    def send(src, dst, ss, rs, peer):
+        copy = pltpu.make_async_remote_copy(
+            src_ref=src, dst_ref=dst, send_sem=ss, recv_sem=rs,
+            device_id=peer, device_id_type=pl.DeviceIdType.MESH,
+        )
+        copy.start()
+        sent.append(copy)
+        return copy
+
+    sent = []
+
+    barrier = pltpu.get_barrier_semaphore()
+    for k in range(1, reps):
+        pl.semaphore_signal(barrier, inc=1, device_id={"rep": rep_peer(k)}, device_id_type=pl.DeviceIdType.MESH)
+    for k in range(1, tps):
+        pl.semaphore_signal(barrier, inc=1, device_id={"tp": tp_peer(k)}, device_id_type=pl.DeviceIdType.MESH)
+
+    def combined_block(owner):
+        at = pl.ds(pl.multiple_of(owner * rows, rows), rows)
+        return grad_ref[at, :].astype(jnp.float32) + feed_ref[at, :]
+
+    order = list(range(1, lines)) + [0]
+    for d in order:
+        pair_send[d] = combined_block(line_at(d) * 2 + (1 - near)).astype(jnp.bfloat16)
+    base_all[me] = (master_ref[...] - (LEARN_RATE * MOMENTUM_RATE) * mom_ref[...]).astype(jnp.bfloat16)
+    vec_all[me] = vgrad_ref[...]
+    pl.semaphore_wait(barrier, reps - 1 + tps - 1)
+
+    pairs = {}
+    for d in order:
+        pairs[d] = send(pair_send.at[d], pair_recv.at[d], pair_ss.at[d], pair_rs.at[d], {"rep": partner})
+    line_copies = []
+    for d in range(1, lines):
+        mine = combined_block(line_at(d) * 2 + near)
+        pairs[d].wait_recv()
+        line_send[d] = (mine + pair_recv[d].astype(jnp.float32)).astype(jnp.bfloat16)
+        line_copies.append(
+            send(line_send.at[d], line_recv.at[d], line_ss.at[d], line_rs.at[d], {"rep": line_at(d) * 2 + near})
+        )
+    base_copies = [None]
+    for d in range(1, lines):
+        base_copies.append(
+            send(base_all.at[me], base_all.at[me], base_ss.at[d], base_rs.at[d], {"rep": line_at(d) * 2 + near})
+        )
+    fwd_copies = [send(base_all.at[me], base_all.at[me], fwd_ss.at[0], fwd_rs.at[0], {"rep": partner})]
+    vec_copies = []
+    for k in range(1, reps):
+        vec_copies.append(send(vec_all.at[me], vec_all.at[me], vec_ss.at[k], vec_rs.at[k], {"rep": rep_peer(k)}))
+    warm_t = warm_ref[...].T
+    total = combined_block(me)
+    pairs[0].wait_recv()
+    total = total + pair_recv[0].astype(jnp.float32)
+    for d in range(1, lines):
+        line_copies[d - 1].wait_recv()
+        total = total + line_recv[d].astype(jnp.float32)
+    sum_high, sum_low = split(total)
+
+    def left_total(phase, factor_t):
+        part = times_parts(factor_t, sum_high, sum_low, NT)
+        tp_send[phase] = part
+        copies = []
+        for k in range(1, tps):
+            copies.append(
+                send(tp_send.at[phase], tp_recv.at[phase, k], tp_ss.at[phase, k], tp_rs.at[phase, k], {"tp": tp_peer(k)})
+            )
+        for k in range(1, tps):
+            copies[k - 1].wait_recv()
+            part = part + tp_recv[phase, k]
+        return part
+
+    def right_total(phase, left_t):
+        left_all[phase, me] = left_t
+        right_t = times_parts(left_t, sum_high, sum_low, NN)
+        for s in range(cols // LANES):
+            for q in range(half):
+                piece_send[phase, s * half + q] = right_t[
+                    q * SUBLANES : (q + 1) * SUBLANES, s * LANES : (s + 1) * LANES
+                ]
+        pieces, lefts, rights = [], [], []
+        for k in range(1, reps):
+            pieces.append(
+                send(
+                    piece_send.at[phase, rep_peer(k)], piece_recv.at[phase, k],
+                    piece_ss.at[phase, k], piece_rs.at[phase, k], {"rep": rep_peer(k)},
+                )
+            )
+        for k in range(1, reps):
+            lefts.append(
+                send(
+                    left_all.at[phase, me], left_all.at[phase, me],
+                    left_ss.at[phase, k], left_rs.at[phase, k], {"rep": rep_peer(k)},
+                )
+            )
+        piece = piece_send[phase, me]
+        for k in range(1, reps):
+            pieces[k - 1].wait_recv()
+            piece = piece + piece_recv[phase, k]
+        right_all[phase, me] = piece
+        for k in range(1, reps):
+            rights.append(
+                send(
+                    right_all.at[phase, me], right_all.at[phase, me],
+                    right_ss.at[phase, k], right_rs.at[phase, k], {"rep": rep_peer(k)},
+                )
+            )
+        for copy in lefts:
+            copy.wait_recv()
+        left_full = jnp.concatenate([left_all[phase, r] for r in range(reps)], axis=1)
+        unlower = inverse_lower(gram_of(left_full))
+
+        def finish():
+            for copy in rights:
+                copy.wait_recv()
+            raw = jnp.concatenate(
+                [
+                    jnp.concatenate([right_all[phase, s * half + q] for q in range(half)], axis=0)
+                    for s in range(cols // LANES)
+                ],
+                axis=1,
+            )
+            return jnp.dot(unlower, raw, precision=PRECISE, preferred_element_type=jnp.float32)
+
+        return left_full, unlower, finish
+
+    left_one = left_total(0, warm_t)
+    _, _, finish_one = right_total(0, left_one)
+    right_one = finish_one()
+    for d in range(1, lines):
+        base_copies[d].wait_recv()
+        slot = lax.rem(far + lines - d, lines) * 2 + near
+        fwd_copies.append(send(base_all.at[slot], base_all.at[slot], fwd_ss.at[d], fwd_rs.at[d], {"rep": partner}))
+    left_two = left_total(1, right_one)
+    left_full, unlower, finish_two = right_total(1, left_two)
+    un_high, un_low = split(unlower)
+    left_high, left_low = split(left_full)
+    ortho = dot16(
+        jnp.concatenate([un_high, un_low, un_high], axis=1),
+        jnp.concatenate([left_high, left_high, left_low], axis=0),
+        NN,
+    )
+    ortho_high, ortho_low = split(ortho)
+    ortho_cat = jnp.concatenate([ortho_high, ortho_low, ortho_high], axis=0)
+    for r in range(reps):
+        ortho_parts[r] = ortho_cat[:, r * rows : (r + 1) * rows]
+
+    for copy in vec_copies:
+        copy.wait_recv()
+    vec_sum = vec_all[0]
+    for r in range(1, reps):
+        vec_sum = vec_sum + vec_all[r]
+    vec_mom = MOMENTUM_RATE * vmom_ref[...] + vec_sum / reps
+    new_vmom_ref[...] = vec_mom
+    new_vpar_ref[...] = vpar_ref[...] - LEARN_RATE * vec_mom
+    for copy in fwd_copies:
+        copy.wait_recv()
+
+    right_high, right_low = split(finish_two() / reps)
+    right_cat = jnp.concatenate([right_high, right_high, right_low], axis=0)
+    for r in range(reps):
+        at = slice(r * rows, (r + 1) * rows)
+        approx = dot16(ortho_parts[r], right_cat, TN)
+        new_feed_ref[at, :] = grad_ref[at, :].astype(jnp.float32) + feed_ref[at, :] - approx
+        weight_ref[at, :] = (base_all[r].astype(jnp.float32) - LEARN_RATE * approx).astype(jnp.bfloat16)
+    own = dot16(ortho_parts[me], right_cat, TN)
+    momentum = MOMENTUM_RATE * mom_ref[...] + own
+    new_mom_ref[...] = momentum
+    new_master_ref[...] = master_ref[...] - LEARN_RATE * momentum
+    for copy in sent:
+        copy.wait_send()
+
+
+def kernel_shards(
+    reps, tps, gradients, feedback, warm_factor, momentum, master_owned, vector_grads, vector_params, vector_momentum
+):
+    rows, cols = momentum.shape
+    rank = warm_factor.shape[1]
+    vec = vector_params.shape[0]
+    lines = reps // 2
+    f32, bf16 = jnp.float32, jnp.bfloat16
+    dma = pltpu.SemaphoreType.DMA
+    vmem = pl.BlockSpec(memory_space=pltpu.VMEM)
+    outs = pl.pallas_call(
+        functools.partial(step_kernel, reps, tps),
+        out_shape=(
+            jax.ShapeDtypeStruct(feedback.shape[1:], f32),
+            jax.ShapeDtypeStruct((rows, cols), f32),
+            jax.ShapeDtypeStruct((rows, cols), f32),
+            jax.ShapeDtypeStruct(feedback.shape[1:], bf16),
+            jax.ShapeDtypeStruct((1, vec), f32),
+            jax.ShapeDtypeStruct((1, vec), f32),
+        ),
+        in_specs=[vmem] * 8,
+        out_specs=(vmem,) * 6,
+        scratch_shapes=[
+            pltpu.VMEM((lines, rows, cols), bf16),
+            pltpu.VMEM((lines, rows, cols), bf16),
+            pltpu.VMEM((lines, rows, cols), bf16),
+            pltpu.VMEM((lines, rows, cols), bf16),
+            pltpu.VMEM((reps, rows, cols), bf16),
+            pltpu.VMEM((2, rank, rows), f32),
+            pltpu.VMEM((2, tps, rank, rows), f32),
+            pltpu.VMEM((2, reps, rank, rows), f32),
+            pltpu.VMEM((2, reps, SUBLANES, LANES), f32),
+            pltpu.VMEM((2, reps, SUBLANES, LANES), f32),
+            pltpu.VMEM((2, reps, SUBLANES, LANES), f32),
+            pltpu.VMEM((reps, 1, vec), f32),
+            pltpu.VMEM((reps, 3 * rank, rows), bf16),
+            dma((lines,)), dma((lines,)),
+            dma((lines,)), dma((lines,)),
+            dma((lines,)), dma((lines,)),
+            dma((lines,)), dma((lines,)),
+            dma((2, tps)), dma((2, tps)),
+            dma((2, reps)), dma((2, reps)),
+            dma((2, reps)), dma((2, reps)),
+            dma((2, reps)), dma((2, reps)),
+            dma((reps,)), dma((reps,)),
+        ],
+        compiler_params=pltpu.CompilerParams(
+            collective_id=0, has_side_effects=True, vmem_limit_bytes=40 * 1024 * 1024
+        ),
+    )(
+        gradients[0], feedback[0], warm_factor, momentum, master_owned,
+        vector_grads, vector_params[None], vector_momentum[None],
+    )
+    new_feedback, new_momentum, new_master, weight, new_params, new_vmom = outs
+    return (new_feedback[None], new_momentum, new_master, weight, new_params[0], new_vmom[0])
+
+
+def step(reps, tps, *arrays):
+    rows, cols = arrays[3].shape
+    rank = arrays[2].shape[1]
+    pieces = (cols // LANES) * (rank // SUBLANES)
+    if reps == pieces and reps % 2 == 0 and rows == LANES:
+        return kernel_shards(reps, tps, *arrays)
+    return shards(*arrays)
+
+
 def solution(mesh):
     return jax.shard_map(
-        shards,
+        functools.partial(step, mesh.shape["rep"], mesh.shape["tp"]),
         mesh=mesh,
         in_specs=(
             P("rep", None, "tp"),

time: 400 us -> 56.3 us (0.14)
  waiting for transfers between devices: 246 us -> 0 us
  blocking collectives: 107 us -> 0 us
  Pallas kernels: 0 us -> 45.4 us
  other arithmetic: 15.9 us -> 1.26 us
  matrix products: 13.6 us -> 0 us
  between operations: 14.2 us -> 0.68 us
  local copies, waits for them, and re-layouts: 2.36 us -> 8.57 us
    psum x2 -> x0, waiting for transfers between devices: 246 us -> none  [left_factor(): return lax.psum(partial_terms, ('rep', 'tp'))]
    psum x2 -> x0, blocking collectives: 75.3 us -> none  [the longest x1 37.9 us: shards(): right_two = lax.psum(right_terms(combined, ortho_two), 'rep')]
    pallas_call x0 -> x1, Pallas kernels: none -> 45.4 us  [kernel_shards(): pl.pallas_call(functools.partial(step_kernel, reps, tps), out_shape=(jax....]
    all_gather x1 -> x0, blocking collectives: 31.4 us -> none  [shards(): lax.all_gather(new_master.astype(jnp.bfloat16), 'rep', axis=0, tiled=True)]
    another operation x10 -> x0, other arithmetic: 13.4 us -> none  [the longest x6 7.19 us: orthonormal(): lower = jnp.linalg.cholesky(gram)]
    dot_general x7 -> x0, matrix products: 12 us -> none  [the longest x2 4.93 us: left_factor(): partial_terms = jnp.dot(combined, factor, precision=PRECISE)]
    unnamed x19 -> x15, local copies, waits for them, and re-layouts: 2.22 us -> 7.11 us
  transfers between devices with their start and end apart: 2 -> 0, of which waited for: 2 -> 0; matrix products, arithmetic and copies ran while one was open for 0% -> 0% of each run, Pallas kernels for 0% -> 0%
where the time goes in v1:
time: 56.3 us; the launch traced here: 55.9 us
  Pallas kernels  45.4 us (81%)
  local copies, waits for them, and re-layouts  8.57 us (15%)
  other arithmetic  1.26 us (2%)
  between operations  0.68 us (1%)
    pallas_call x1, Pallas kernels, kernel_shards(): pl.pallas_call(functools.partial(step_kernel, reps, tps), out_shape=(jax....  45.4 us
    unnamed x15, local copies, waits for them, and re-layouts  7.11 us
    pallas_call x2, other arithmetic, kernel_shards(): pl.pallas_call(functools.partial(step_kernel, reps, tps), out_shape=(jax....  1.26 us

profile of v1, /device:TPU:0, one launch (start us, length us, event | category | flops | bytes accessed | tf_op | source)
XLA Modules:
  0.0 55.9 jit_solution(5546389072200386028)
XLA Ops:
  0.6 0.0 copy-start.2
  0.6 0.8 %broadcast_in_dim.9.vpar_ref = f32[1,2560]{1,0:T(1,128)S(1)} reshape(f32[2560]{0:T(1024)} %param.14) | data formatting | bytes 20480 | tf_op jit(solution)/shard_map/broadcast_in_dim | solution.py:400
  1.4 0.7 %broadcast_in_dim.10.vmom_ref = f32[1,2560]{1,0:T(1,128)S(1)} reshape(f32[2560]{0:T(1024)} %param.15) | data formatting | bytes 20480 | tf_op jit(solution)/shard_map/broadcast_in_dim | solution.py:400
  2.1 0.0 copy-start.4
  2.1 0.9 %copy.14.warm_ref = f32[256,32]{1,0:T(8,128)S(1)} copy(f32[256,32]{0,1:T(8,128)} %param.10) | data formatting | bytes 65536 | tf_op args[2]
  3.0 0.0 copy-done.2
  3.0 0.0 copy-done.4
  3.0 0.0 copy-start
  3.0 1.2 %copy-done = f32[1,1024,256]{2,1,0:T(8,128)S(1)} copy-done((f32[1,1024,256]{2,1,0:T(8,128)S(1)}, f32[1,1024,256]{2,1,0:T(8,128)}, u32[]{:S(2)}) %copy-start) | copy-done | bytes 1048600
  4.2 0.0 copy-start.1
  4.2 1.0 %copy-done.1 = bf16[1,1024,256]{2,1,0:T(8,128)(2,1)S(1)} copy-done((bf16[1,1024,256]{2,1,0:T(8,128)(2,1)S(1)}, bf16[1,1024,256]{2,1,0:T(8,128)(2,1)}, u32[]{:S(2)}) %copy-start.1) | copy-done | bytes 524312
  5.3 0.0 copy-start.3
  5.3 0.9 %copy-done.3 = f32[128,256]{1,0:T(8,128)S(1)} copy-done((f32[128,256]{1,0:T(8,128)S(1)}, f32[128,256]{1,0:T(8,128)}, u32[]{:S(2)}) %copy-start.3) | copy-done | bytes 131096
  6.2 45.4 %shard_map.127 = (f32[1024,256]{1,0:T(8,128)S(1)}, f32[128,256]{1,0:T(8,128)S(1)}, f32[128,256]{1,0:T(8,128)S(1)}, bf16[1024,256]{1,0:T(8,128)(2,1)S(1)}, f32[1,2560]{1,0:T(1,128)S(1)}, /*index=5*/f32[1,2560]{1,0:T(1,128)S(1)}) custom-call(bf16[1024,256]{1,0:T(8,128)(2,1)S(1)} %bitcast.5, f32[1024,256]{1,0:T(8,128)S(1)} %bitcast.3, ...), custom_call_target="tpu_custom_call" | custom-call | tf_op jit(solution)/shard_map/pallas_call | solution.py:359
  51.6 0.6 %reduce = f32[2560]{0:T(1024)} reduce(f32[1,2560]{1,0:T(1,128)S(1)} %get-tuple-element.16, f32[]{:T(128)} %constant.3), dimensions={0}, to_apply=%get-tuple-element.16.reduce_sub_computation | reduce | bytes 20484 | tf_op jit(solution)/shard_map/pallas_call | solution.py:359
  52.2 0.6 %reduce.1 = f32[2560]{0:T(1024)} reduce(f32[1,2560]{1,0:T(1,128)S(1)} %get-tuple-element.17, f32[]{:T(128)} %constant.3), dimensions={0}, to_apply=%get-tuple-element.17.reduce_sub_computation | reduce | bytes 20484 | tf_op jit(solution)/shard_map/pallas_call | solution.py:359
  52.8 1.0 %copy.19 = f32[1,1024,256]{2,1,0:T(8,128)} copy(f32[1,1024,256]{2,1,0:T(8,128)S(1)} %bitcast.4) | data formatting | bytes 2097152
  53.8 0.7 %copy.20 = f32[128,256]{1,0:T(8,128)} copy(f32[128,256]{1,0:T(8,128)S(1)} %get-tuple-element.25) | data formatting | bytes 262144
  54.5 0.7 %copy.21 = f32[128,256]{1,0:T(8,128)} copy(f32[128,256]{1,0:T(8,128)S(1)} %get-tuple-element.26) | data formatting | bytes 262144
  55.1 0.8 %copy.22 = bf16[1024,256]{1,0:T(8,128)(2,1)} copy(bf16[1024,256]{1,0:T(8,128)(2,1)S(1)} %get-tuple-element.27) | data formatting | bytes 1048576
Async XLA Ops:
  0.6 2.3 %copy-start.2 = (f32[128,256]{1,0:T(8,128)S(1)}, f32[128,256]{1,0:T(8,128)}, u32[]{:S(2)}) copy-start(f32[128,256]{1,0:T(8,128)} %mom_ref.1) | copy-start | bytes 393220
  2.1 0.9 %copy-start.4 = (f32[1,2560]{1,0:T(1,128)S(1)}, f32[1,2560]{1,0:T(1,128)}, u32[]{:S(2)}) copy-start(f32[1,2560]{1,0:T(1,128)} %vgrad_ref.1) | copy-start | bytes 30724
  3.0 1.2 %copy-start = (f32[1,1024,256]{2,1,0:T(8,128)S(1)}, f32[1,1024,256]{2,1,0:T(8,128)}, u32[]{:S(2)}) copy-start(f32[1,1024,256]{2,1,0:T(8,128)} %param.9) | copy-start | bytes 3145732
  4.2 1.0 %copy-start.1 = (bf16[1,1024,256]{2,1,0:T(8,128)(2,1)S(1)}, bf16[1,1024,256]{2,1,0:T(8,128)(2,1)}, u32[]{:S(2)}) copy-start(bf16[1,1024,256]{2,1,0:T(8,128)(2,1)} %param.8) | copy-start | bytes 1572868
  5.3 0.9 %copy-start.3 = (f32[128,256]{1,0:T(8,128)S(1)}, f32[128,256]{1,0:T(8,128)}, u32[]{:S(2)}) copy-start(f32[128,256]{1,0:T(8,128)} %master_ref.1) | copy-start | bytes 393220

commit v2 on v1

--- a/solution.py
+++ b/solution.py
@@ -96,35 +96,55 @@
 
 def inverse_lower(gram):
     rank = gram.shape[0]
-    row_id = lax.broadcasted_iota(jnp.int32, (rank, 2 * rank), 0)
-    lane_id = lax.broadcasted_iota(jnp.int32, (rank, 2 * rank), 1)
+    count = rank // SUBLANES
+    row_id = lax.broadcasted_iota(jnp.int32, (rank, LANES), 0)
+    lane_id = lax.broadcasted_iota(jnp.int32, (rank, LANES), 1)
     unit = (lane_id == row_id + rank).astype(jnp.float32)
     work = jnp.concatenate([gram, unit[:, rank:]], axis=1)
-    for j in range(rank):
-        scale = lax.rsqrt(work[j : j + 1, j : j + 1])
-        row = work[j : j + 1, :] * scale
-        column = work[:, j : j + 1] * scale
-        work = jnp.where(row_id < j, work, jnp.where(row_id == j, row, work - column * row))
-    return work[:, rank:]
+    tiles = [work[q * SUBLANES : (q + 1) * SUBLANES] for q in range(count)]
+    tile_row = row_id[:SUBLANES]
+    done = []
+    for g in range(count):
+        spread = [
+            [jnp.broadcast_to(tiles[q][:, k : k + 1], (SUBLANES, LANES)) for q in range(g, count)]
+            for k in range(g * SUBLANES, (g + 1) * SUBLANES)
+        ]
+        out = tiles[g]
+        for j in range(SUBLANES):
+            scale = lax.rsqrt(spread[j][0][j : j + 1])
+            row = tiles[g][j : j + 1] * scale
+            out = jnp.where(tile_row == j, row, out)
+            column = [part * scale for part in spread[j]]
+            for k in range(j + 1, SUBLANES):
+                cross = spread[k][0][j : j + 1] * scale
+                spread[k] = [part - c * cross for part, c in zip(spread[k], column)]
+            for q in range(g, count):
+                tiles[q] = tiles[q] - column[q - g] * row
+        done.append(out)
+    return jnp.concatenate(done, axis=0)[:, rank : 2 * rank]
 
 
 def step_kernel(
     reps,
     tps,
+    grad_hbm,
+    feed_hbm,
+    warm_hbm,
+    mom_hbm,
+    master_hbm,
+    vgrad_hbm,
+    comb_ref,
+    ortho_ref,
+    right_ref,
+    base_ref,
+    vsum_ref,
     grad_ref,
     feed_ref,
     warm_ref,
     mom_ref,
     master_ref,
     vgrad_ref,
-    vpar_ref,
-    vmom_ref,
-    new_feed_ref,
-    new_mom_ref,
-    new_master_ref,
-    weight_ref,
-    new_vpar_ref,
-    new_vmom_ref,
+    load_sem,
     pair_send,
     pair_recv,
     line_send,
@@ -137,7 +157,6 @@
     piece_recv,
     right_all,
     vec_all,
-    ortho_parts,
     pair_ss,
     pair_rs,
     line_ss,
@@ -163,7 +182,7 @@
     far, near = me // 2, me % 2
     partner = far * 2 + (1 - near)
     rows, cols = mom_ref.shape
-    rank = warm_ref.shape[1]
+    rank = warm_ref.shape[0]
     half = rank // SUBLANES
 
     def rep_peer(k):
@@ -185,6 +204,19 @@
         return copy
 
     sent = []
+    loads = []
+    for i, (src, dst) in enumerate(
+        (
+            (grad_hbm, grad_ref),
+            (feed_hbm, feed_ref),
+            (mom_hbm, mom_ref),
+            (master_hbm, master_ref),
+            (warm_hbm, warm_ref),
+            (vgrad_hbm, vgrad_ref),
+        )
+    ):
+        loads.append(pltpu.make_async_copy(src, dst, load_sem.at[i]))
+        loads[i].start()
 
     barrier = pltpu.get_barrier_semaphore()
     for k in range(1, reps):
@@ -194,18 +226,24 @@
 
     def combined_block(owner):
         at = pl.ds(pl.multiple_of(owner * rows, rows), rows)
-        return grad_ref[at, :].astype(jnp.float32) + feed_ref[at, :]
+        block = grad_ref[at, :].astype(jnp.float32) + feed_ref[at, :]
+        comb_ref[at, :] = block
+        return block
 
     order = list(range(1, lines)) + [0]
+    loads[0].wait()
+    loads[1].wait()
     for d in order:
         pair_send[d] = combined_block(line_at(d) * 2 + (1 - near)).astype(jnp.bfloat16)
-    base_all[me] = (master_ref[...] - (LEARN_RATE * MOMENTUM_RATE) * mom_ref[...]).astype(jnp.bfloat16)
-    vec_all[me] = vgrad_ref[...]
     pl.semaphore_wait(barrier, reps - 1 + tps - 1)
 
     pairs = {}
     for d in order:
         pairs[d] = send(pair_send.at[d], pair_recv.at[d], pair_ss.at[d], pair_rs.at[d], {"rep": partner})
+    for copy in loads[2:]:
+        copy.wait()
+    base_all[me] = (master_ref[...] - (LEARN_RATE * MOMENTUM_RATE) * mom_ref[...]).astype(jnp.bfloat16)
+    vec_all[me] = vgrad_ref[...]
     line_copies = []
     for d in range(1, lines):
         mine = combined_block(line_at(d) * 2 + near)
@@ -223,7 +261,6 @@
     vec_copies = []
     for k in range(1, reps):
         vec_copies.append(send(vec_all.at[me], vec_all.at[me], vec_ss.at[k], vec_rs.at[k], {"rep": rep_peer(k)}))
-    warm_t = warm_ref[...].T
     total = combined_block(me)
     pairs[0].wait_recv()
     total = total + pair_recv[0].astype(jnp.float32)
@@ -299,7 +336,7 @@
 
         return left_full, unlower, finish
 
-    left_one = left_total(0, warm_t)
+    left_one = left_total(0, warm_ref[...])
     _, _, finish_one = right_total(0, left_one)
     right_one = finish_one()
     for d in range(1, lines):
@@ -318,32 +355,94 @@
     ortho_high, ortho_low = split(ortho)
     ortho_cat = jnp.concatenate([ortho_high, ortho_low, ortho_high], axis=0)
     for r in range(reps):
-        ortho_parts[r] = ortho_cat[:, r * rows : (r + 1) * rows]
+        ortho_ref[r] = ortho_cat[:, r * rows : (r + 1) * rows].T
 
     for copy in vec_copies:
         copy.wait_recv()
     vec_sum = vec_all[0]
     for r in range(1, reps):
         vec_sum = vec_sum + vec_all[r]
-    vec_mom = MOMENTUM_RATE * vmom_ref[...] + vec_sum / reps
-    new_vmom_ref[...] = vec_mom
-    new_vpar_ref[...] = vpar_ref[...] - LEARN_RATE * vec_mom
+    vsum_ref[...] = vec_sum
     for copy in fwd_copies:
         copy.wait_recv()
+    for r in range(reps):
+        base_ref[r] = base_all[r]
+    for copy in sent[: len(sent) - (reps - 1)]:
+        copy.wait_send()
 
     right_high, right_low = split(finish_two() / reps)
-    right_cat = jnp.concatenate([right_high, right_high, right_low], axis=0)
+    right_ref[...] = jnp.concatenate([right_high, right_high, right_low], axis=0)
+    for copy in sent[len(sent) - (reps - 1) :]:
+        copy.wait_send()
+
+
+def finish_kernel(
+    reps,
+    comb_ref,
+    ortho_ref,
+    right_ref,
+    base_ref,
+    vsum_ref,
+    mom_hbm,
+    master_hbm,
+    vpar_hbm,
+    vmom_hbm,
+    new_feed_hbm,
+    new_mom_hbm,
+    new_master_hbm,
+    weight_hbm,
+    new_vpar_hbm,
+    new_vmom_hbm,
+    mom_ref,
+    master_ref,
+    vpar_ref,
+    vmom_ref,
+    feed_ref,
+    weight_ref,
+    load_sem,
+    feed_sem,
+    weight_sem,
+    out_sem,
+):
+    me = lax.axis_index("rep")
+    rows = mom_ref.shape[0]
+    loads = []
+    for i, (src, dst) in enumerate(
+        ((mom_hbm, mom_ref), (master_hbm, master_ref), (vpar_hbm, vpar_ref), (vmom_hbm, vmom_ref))
+    ):
+        loads.append(pltpu.make_async_copy(src, dst, load_sem.at[i]))
+        loads[i].start()
+    stores = []
+
+    def store(src, dst, sem):
+        stores.append(pltpu.make_async_copy(src, dst, sem))
+        stores[-1].start()
+
+    right = right_ref[...]
     for r in range(reps):
-        at = slice(r * rows, (r + 1) * rows)
-        approx = dot16(ortho_parts[r], right_cat, TN)
-        new_feed_ref[at, :] = grad_ref[at, :].astype(jnp.float32) + feed_ref[at, :] - approx
-        weight_ref[at, :] = (base_all[r].astype(jnp.float32) - LEARN_RATE * approx).astype(jnp.bfloat16)
-    own = dot16(ortho_parts[me], right_cat, TN)
+        at = pl.ds(r * rows, rows)
+        approx = dot16(ortho_ref[r], right, NN)
+        feed_ref[at, :] = comb_ref[at, :] - approx
+        store(feed_ref.at[at, :], new_feed_hbm.at[at, :], feed_sem.at[r])
+        weight_ref[at, :] = (base_ref[r].astype(jnp.float32) - LEARN_RATE * approx).astype(jnp.bfloat16)
+        store(weight_ref.at[at, :], weight_hbm.at[at, :], weight_sem.at[r])
+    own = dot16(ortho_ref[me], right, NN)
+    for copy in loads:
+        copy.wait()
     momentum = MOMENTUM_RATE * mom_ref[...] + own
-    new_mom_ref[...] = momentum
-    new_master_ref[...] = master_ref[...] - LEARN_RATE * momentum
-    for copy in sent:
-        copy.wait_send()
+    mom_ref[...] = momentum
+    store(mom_ref, new_mom_hbm, out_sem.at[0])
+    master_ref[...] = master_ref[...] - LEARN_RATE * momentum
+    store(master_ref, new_master_hbm, out_sem.at[1])
+    for c in range(vsum_ref.shape[1] // LANES):
+        at = pl.ds(c * LANES, LANES)
+        vec = MOMENTUM_RATE * vmom_ref[at] + vsum_ref[0, at] / reps
+        vmom_ref[at] = vec
+        vpar_ref[at] = vpar_ref[at] - LEARN_RATE * vec
+    store(vpar_ref, new_vpar_hbm, out_sem.at[2])
+    store(vmom_ref, new_vmom_hbm, out_sem.at[3])
+    for copy in stores:
+        copy.wait()
 
 
 def kernel_shards(
@@ -356,19 +455,28 @@
     f32, bf16 = jnp.float32, jnp.bfloat16
     dma = pltpu.SemaphoreType.DMA
     vmem = pl.BlockSpec(memory_space=pltpu.VMEM)
-    outs = pl.pallas_call(
+    hbm = pl.BlockSpec(memory_space=pltpu.HBM)
+    whole = feedback.shape[1:]
+    shape = jax.ShapeDtypeStruct
+    parts = pl.pallas_call(
         functools.partial(step_kernel, reps, tps),
         out_shape=(
-            jax.ShapeDtypeStruct(feedback.shape[1:], f32),
-            jax.ShapeDtypeStruct((rows, cols), f32),
-            jax.ShapeDtypeStruct((rows, cols), f32),
-            jax.ShapeDtypeStruct(feedback.shape[1:], bf16),
-            jax.ShapeDtypeStruct((1, vec), f32),
-            jax.ShapeDtypeStruct((1, vec), f32),
+            shape(whole, f32),
+            shape((reps, rows, 3 * rank), bf16),
+            shape((3 * rank, cols), bf16),
+            shape((reps, rows, cols), bf16),
+            shape((1, vec), f32),
         ),
-        in_specs=[vmem] * 8,
-        out_specs=(vmem,) * 6,
+        in_specs=[hbm] * 6,
+        out_specs=(vmem,) * 5,
         scratch_shapes=[
+            pltpu.VMEM(whole, bf16),
+            pltpu.VMEM(whole, f32),
+            pltpu.VMEM((rank, cols), f32),
+            pltpu.VMEM((rows, cols), f32),
+            pltpu.VMEM((rows, cols), f32),
+            pltpu.VMEM((1, vec), f32),
+            dma((6,)),
             pltpu.VMEM((lines, rows, cols), bf16),
             pltpu.VMEM((lines, rows, cols), bf16),
             pltpu.VMEM((lines, rows, cols), bf16),
@@ -381,7 +489,6 @@
             pltpu.VMEM((2, reps, SUBLANES, LANES), f32),
             pltpu.VMEM((2, reps, SUBLANES, LANES), f32),
             pltpu.VMEM((reps, 1, vec), f32),
-            pltpu.VMEM((reps, 3 * rank, rows), bf16),
             dma((lines,)), dma((lines,)),
             dma((lines,)), dma((lines,)),
             dma((lines,)), dma((lines,)),
@@ -396,11 +503,32 @@
             collective_id=0, has_side_effects=True, vmem_limit_bytes=40 * 1024 * 1024
         ),
     )(
-        gradients[0], feedback[0], warm_factor, momentum, master_owned,
-        vector_grads, vector_params[None], vector_momentum[None],
+        gradients[0], feedback[0], warm_factor.T, momentum, master_owned, vector_grads
     )
-    new_feedback, new_momentum, new_master, weight, new_params, new_vmom = outs
-    return (new_feedback[None], new_momentum, new_master, weight, new_params[0], new_vmom[0])
+    outs = pl.pallas_call(
+        functools.partial(finish_kernel, reps),
+        out_shape=(
+            shape(whole, f32),
+            shape((rows, cols), f32),
+            shape((rows, cols), f32),
+            shape(whole, bf16),
+            shape((vec,), f32),
+            shape((vec,), f32),
+        ),
+        in_specs=[vmem] * 5 + [hbm] * 4,
+        out_specs=(hbm,) * 6,
+        scratch_shapes=[
+            pltpu.VMEM((rows, cols), f32),
+            pltpu.VMEM((rows, cols), f32),
+            pltpu.VMEM((vec,), f32),
+            pltpu.VMEM((vec,), f32),
+            pltpu.VMEM(whole, f32),
+            pltpu.VMEM(whole, bf16),
+            dma((4,)), dma((reps,)), dma((reps,)), dma((4,)),
+        ],
+        compiler_params=pltpu.CompilerParams(vmem_limit_bytes=40 * 1024 * 1024),
+    )(*parts, momentum, master_owned, vector_params, vector_momentum)
+    return (outs[0][None],) + tuple(outs[1:])
 
 
 def step(reps, tps, *arrays):

time: 56.3 us -> 53.8 us (0.956)
  local copies, waits for them, and re-layouts: 8.57 us -> 5.54 us
  Pallas kernels: 45.4 us -> 47.3 us
  other arithmetic: 1.26 us -> 0 us
    pallas_call x1 -> x2, Pallas kernels: 45.4 us -> 47.3 us  [the longest x1 45.3 us: kernel_shards(): pl.pallas_call(functools.partial(step_kernel, reps, tps), out_shape=(shap...]
    unnamed x15 -> x18, local copies, waits for them, and re-layouts: 7.11 us -> 5.54 us
    broadcast_in_dim x2 -> x0, local copies, waits for them, and re-layouts: 1.46 us -> none  [the longest x1 0.75 us: kernel_shards(): vector_params[None]]
    pallas_call x2 -> x0, other arithmetic: 1.26 us -> none  [kernel_shards(): pl.pallas_call(functools.partial(step_kernel, reps, tps), out_shape=(jax....]
where the time goes in v2:
time: 53.8 us; the launch traced here: 53.5 us
  Pallas kernels  47.3 us (88%)
  local copies, waits for them, and re-layouts  5.54 us (10%)
  between operations  0.68 us (1%)
    pallas_call x1, Pallas kernels, kernel_shards(): pl.pallas_call(functools.partial(step_kernel, reps, tps), out_shape=(shap...  45.3 us
    unnamed x18, local copies, waits for them, and re-layouts  5.54 us
    pallas_call x1, Pallas kernels, kernel_shards(): pl.pallas_call(functools.partial(finish_kernel, reps), out_shape=(shape(w...  1.96 us

profile of v2, /device:TPU:0, one launch (start us, length us, event | category | flops | bytes accessed | tf_op | source)
XLA Modules:
  0.0 53.5 jit_solution(17412310914728939715)
XLA Ops:
  0.6 0.0 copy-start
  0.6 1.2 %copy-done = f32[1,1024,256]{2,1,0:T(8,128)S(1)} copy-done((f32[1,1024,256]{2,1,0:T(8,128)S(1)}, f32[1,1024,256]{2,1,0:T(8,128)}, u32[]{:S(2)}) %copy-start) | copy-done | bytes 1048600
  1.9 0.0 copy-start.1
  1.9 1.0 %copy-done.1 = bf16[1,1024,256]{2,1,0:T(8,128)(2,1)S(1)} copy-done((bf16[1,1024,256]{2,1,0:T(8,128)(2,1)S(1)}, bf16[1,1024,256]{2,1,0:T(8,128)(2,1)}, u32[]{:S(2)}) %copy-start.1) | copy-done | bytes 524312
  2.9 0.0 copy-start.2
  2.9 0.9 %copy-done.2 = f32[128,256]{1,0:T(8,128)S(1)} copy-done((f32[128,256]{1,0:T(8,128)S(1)}, f32[128,256]{1,0:T(8,128)}, u32[]{:S(2)}) %copy-start.2) | copy-done | bytes 131096
  3.8 0.0 copy-start.4
  3.8 0.9 %copy-done.4 = f32[128,256]{1,0:T(8,128)S(1)} copy-done((f32[128,256]{1,0:T(8,128)S(1)}, f32[128,256]{1,0:T(8,128)}, u32[]{:S(2)}) %copy-start.4) | copy-done | bytes 131096
  4.7 0.0 copy-start.5
  4.7 0.8 %copy-done.5 = f32[256,32]{0,1:T(8,128)S(1)} copy-done((f32[256,32]{0,1:T(8,128)S(1)}, f32[256,32]{0,1:T(8,128)}, u32[]{:S(2)}) %copy-start.5) | copy-done | bytes 32792
  5.5 0.0 copy-start.8
  5.5 0.7 %copy-done.8 = f32[1,2560]{1,0:T(1,128)S(1)} copy-done((f32[1,2560]{1,0:T(1,128)S(1)}, f32[1,2560]{1,0:T(1,128)}, u32[]{:S(2)}) %copy-start.8) | copy-done | bytes 10264
  6.2 0.0 copy-start.3
  6.2 0.0 copy-start.6
  6.2 0.0 copy-start.7
  6.2 45.3 %shard_map.127 = (f32[1024,256]{1,0:T(8,128)S(1)}, bf16[8,128,96]{2,1,0:T(8,128)(2,1)S(1)}, bf16[96,256]{1,0:T(8,128)(2,1)S(1)}, bf16[8,128,256]{2,1,0:T(8,128)(2,1)S(1)}, f32[1,2560]{1,0:T(1,128)S(1)}) custom-call(bf16[1024,256]{1,0:T(8,128)(2,1)S(1)} %bitcast.5, f32[1024,256]{1,0:T(8,128)S(1)} %bitcast.4, f32[32,256]{1,0:T(8,128)S(1)} %bitcast.6, ...), custom_call_target="tpu_custom_call" | custom-call | tf_op jit(solution)/shard_map/pallas_call | solution.py:461
  51.5 0.0 copy-done.3
  51.5 0.0 copy-done.6
  51.5 0.0 copy-done.7
  51.5 2.0 %shard_map.128 = (f32[1024,256]{1,0:T(8,128)}, f32[128,256]{1,0:T(8,128)}, f32[128,256]{1,0:T(8,128)}, bf16[1024,256]{1,0:T(8,128)(2,1)}, f32[2560]{0:T(1024)}, /*index=5*/f32[2560]{0:T(1024)}) custom-call(f32[1024,256]{1,0:T(8,128)S(1)} %get-tuple-element.17.comb_ref, bf16[8,128,96]{2,1,0:T(8,128)(2,1)S(1)} %get-tuple-element.18.ortho_ref, ...), custom_call_target="tpu_custom_call" | custom-call | tf_op jit(solution)/shard_map/pallas_call | solution.py:508
Async XLA Ops:
  0.6 1.2 %copy-start = (f32[1,1024,256]{2,1,0:T(8,128)S(1)}, f32[1,1024,256]{2,1,0:T(8,128)}, u32[]{:S(2)}) copy-start(f32[1,1024,256]{2,1,0:T(8,128)} %param.9) | copy-start | bytes 3145732
  1.9 1.0 %copy-start.1 = (bf16[1,1024,256]{2,1,0:T(8,128)(2,1)S(1)}, bf16[1,1024,256]{2,1,0:T(8,128)(2,1)}, u32[]{:S(2)}) copy-start(bf16[1,1024,256]{2,1,0:T(8,128)(2,1)} %param.8) | copy-start | bytes 1572868
  2.9 0.9 %copy-start.2 = (f32[128,256]{1,0:T(8,128)S(1)}, f32[128,256]{1,0:T(8,128)}, u32[]{:S(2)}) copy-start(f32[128,256]{1,0:T(8,128)} %mom_hbm.3) | copy-start | bytes 393220
  3.8 0.9 %copy-start.4 = (f32[128,256]{1,0:T(8,128)S(1)}, f32[128,256]{1,0:T(8,128)}, u32[]{:S(2)}) copy-start(f32[128,256]{1,0:T(8,128)} %master_hbm.3) | copy-start | bytes 393220
  4.7 0.8 %copy-start.5 = (f32[256,32]{0,1:T(8,128)S(1)}, f32[256,32]{0,1:T(8,128)}, u32[]{:S(2)}) copy-start(f32[256,32]{0,1:T(8,128)} %param.10) | copy-start | bytes 98308
  5.5 0.7 %copy-start.8 = (f32[1,2560]{1,0:T(1,128)S(1)}, f32[1,2560]{1,0:T(1,128)}, u32[]{:S(2)}) copy-start(f32[1,2560]{1,0:T(1,128)} %vgrad_hbm.1) | copy-start | bytes 30724
  6.2 45.3 %copy-start.3 = (f32[128,256]{1,0:T(8,128)S(1)}, f32[128,256]{1,0:T(8,128)}, u32[]{:S(2)}) copy-start(f32[128,256]{1,0:T(8,128)} %mom_hbm.3) | copy-start | bytes 393220
  6.2 45.3 %copy-start.6 = (f32[2560]{0:T(1024)S(1)}, f32[2560]{0:T(1024)}, u32[]{:S(2)}) copy-start(f32[2560]{0:T(1024)} %vpar_hbm.1) | copy-start | bytes 30724
  6.2 45.3 %copy-start.7 = (f32[2560]{0:T(1024)S(1)}, f32[2560]{0:T(1024)}, u32[]{:S(2)}) copy-start(f32[2560]{0:T(1024)} %vmom_hbm.1) | copy-start | bytes 30724

commit v3 on v2

--- a/solution.py
+++ b/solution.py
@@ -84,7 +84,7 @@
 
 def gram_of(left_t):
     rank = left_t.shape[0]
-    high, rest = left_t.astype(jnp.bfloat16), None
+    high = left_t.astype(jnp.bfloat16)
     rest = left_t - high.astype(jnp.float32)
     middle = rest.astype(jnp.bfloat16)
     low = (rest - middle.astype(jnp.float32)).astype(jnp.bfloat16)
@@ -92,6 +92,25 @@
     grid = dot16(parts, parts, NT)
     rows = grid[:rank] + grid[rank : 2 * rank] + grid[2 * rank :]
     return rows[:, :rank] + rows[:, rank : 2 * rank] + rows[:, 2 * rank :]
+
+
+def stack_left(a):
+    high, low = split(a)
+    return jnp.concatenate([high, low, high], axis=1)
+
+
+def stack_right(b):
+    high, low = split(b)
+    return jnp.concatenate([high, high, low], axis=0)
+
+
+def pack_square(square):
+    rank = square.shape[0]
+    return jnp.concatenate([square[q : q + SUBLANES] for q in range(0, rank, SUBLANES)], axis=1)
+
+
+def unpack_square(packed, rank):
+    return jnp.concatenate([packed[:, q : q + rank] for q in range(0, LANES, rank)], axis=0)
 
 
 def inverse_lower(gram):
@@ -133,11 +152,14 @@
     mom_hbm,
     master_hbm,
     vgrad_hbm,
-    comb_ref,
+    ortho_hbm,
+    right_hbm,
+    base_hbm,
+    vsum_hbm,
     ortho_ref,
     right_ref,
-    base_ref,
     vsum_ref,
+    out_sem,
     grad_ref,
     feed_ref,
     warm_ref,
@@ -157,6 +179,8 @@
     piece_recv,
     right_all,
     vec_all,
+    vec_tp,
+    gram_all,
     pair_ss,
     pair_rs,
     line_ss,
@@ -175,6 +199,10 @@
     right_rs,
     vec_ss,
     vec_rs,
+    vtp_ss,
+    vtp_rs,
+    gram_ss,
+    gram_rs,
 ):
     me = lax.axis_index("rep")
     col = lax.axis_index("tp")
@@ -226,9 +254,7 @@
 
     def combined_block(owner):
         at = pl.ds(pl.multiple_of(owner * rows, rows), rows)
-        block = grad_ref[at, :].astype(jnp.float32) + feed_ref[at, :]
-        comb_ref[at, :] = block
-        return block
+        return grad_ref[at, :].astype(jnp.float32) + feed_ref[at, :]
 
     order = list(range(1, lines)) + [0]
     loads[0].wait()
@@ -243,7 +269,17 @@
     for copy in loads[2:]:
         copy.wait()
     base_all[me] = (master_ref[...] - (LEARN_RATE * MOMENTUM_RATE) * mom_ref[...]).astype(jnp.bfloat16)
-    vec_all[me] = vgrad_ref[...]
+    quarter = vgrad_ref.shape[1] // tps
+    vec_all[me] = vgrad_ref[:, pl.ds(pl.multiple_of(col * quarter, LANES), quarter)]
+    base_copies = [None]
+
+    def send_base(d):
+        base_copies.append(
+            send(base_all.at[me], base_all.at[me], base_ss.at[d], base_rs.at[d], {"rep": line_at(d) * 2 + near})
+        )
+
+    for d in range(1, lines - 1):
+        send_base(d)
     line_copies = []
     for d in range(1, lines):
         mine = combined_block(line_at(d) * 2 + near)
@@ -252,15 +288,6 @@
         line_copies.append(
             send(line_send.at[d], line_recv.at[d], line_ss.at[d], line_rs.at[d], {"rep": line_at(d) * 2 + near})
         )
-    base_copies = [None]
-    for d in range(1, lines):
-        base_copies.append(
-            send(base_all.at[me], base_all.at[me], base_ss.at[d], base_rs.at[d], {"rep": line_at(d) * 2 + near})
-        )
-    fwd_copies = [send(base_all.at[me], base_all.at[me], fwd_ss.at[0], fwd_rs.at[0], {"rep": partner})]
-    vec_copies = []
-    for k in range(1, reps):
-        vec_copies.append(send(vec_all.at[me], vec_all.at[me], vec_ss.at[k], vec_rs.at[k], {"rep": rep_peer(k)}))
     total = combined_block(me)
     pairs[0].wait_recv()
     total = total + pair_recv[0].astype(jnp.float32)
@@ -269,7 +296,7 @@
         total = total + line_recv[d].astype(jnp.float32)
     sum_high, sum_low = split(total)
 
-    def left_total(phase, factor_t):
+    def left_total(phase, factor_t, meanwhile):
         part = times_parts(factor_t, sum_high, sum_low, NT)
         tp_send[phase] = part
         copies = []
@@ -277,20 +304,21 @@
             copies.append(
                 send(tp_send.at[phase], tp_recv.at[phase, k], tp_ss.at[phase, k], tp_rs.at[phase, k], {"tp": tp_peer(k)})
             )
+        meanwhile()
         for k in range(1, tps):
             copies[k - 1].wait_recv()
             part = part + tp_recv[phase, k]
         return part
 
     def right_total(phase, left_t):
-        left_all[phase, me] = left_t
+        gram_all[phase, me] = pack_square(gram_of(left_t))
         right_t = times_parts(left_t, sum_high, sum_low, NN)
         for s in range(cols // LANES):
             for q in range(half):
                 piece_send[phase, s * half + q] = right_t[
                     q * SUBLANES : (q + 1) * SUBLANES, s * LANES : (s + 1) * LANES
                 ]
-        pieces, lefts, rights = [], [], []
+        pieces, grams, rights = [], [], []
         for k in range(1, reps):
             pieces.append(
                 send(
@@ -299,10 +327,10 @@
                 )
             )
         for k in range(1, reps):
-            lefts.append(
+            grams.append(
                 send(
-                    left_all.at[phase, me], left_all.at[phase, me],
-                    left_ss.at[phase, k], left_rs.at[phase, k], {"rep": rep_peer(k)},
+                    gram_all.at[phase, me], gram_all.at[phase, me],
+                    gram_ss.at[phase, k], gram_rs.at[phase, k], {"rep": rep_peer(k)},
                 )
             )
         piece = piece_send[phase, me]
@@ -317,10 +345,19 @@
                     right_ss.at[phase, k], right_rs.at[phase, k], {"rep": rep_peer(k)},
                 )
             )
-        for copy in lefts:
+        lefts = []
+        if phase == 1:
+            left_all[me] = left_t
+            for k in range(1, reps):
+                lefts.append(
+                    send(left_all.at[me], left_all.at[me], left_ss.at[k], left_rs.at[k], {"rep": rep_peer(k)})
+                )
+        for copy in grams:
             copy.wait_recv()
-        left_full = jnp.concatenate([left_all[phase, r] for r in range(reps)], axis=1)
-        unlower = inverse_lower(gram_of(left_full))
+        gram = gram_all[phase, 0]
+        for r in range(1, reps):
+            gram = gram + gram_all[phase, r]
+        unlower = stack_left(inverse_lower(unpack_square(gram, rank)))
 
         def finish():
             for copy in rights:
@@ -332,57 +369,80 @@
                 ],
                 axis=1,
             )
-            return jnp.dot(unlower, raw, precision=PRECISE, preferred_element_type=jnp.float32)
-
-        return left_full, unlower, finish
-
-    left_one = left_total(0, warm_ref[...])
-    _, _, finish_one = right_total(0, left_one)
-    right_one = finish_one()
-    for d in range(1, lines):
-        base_copies[d].wait_recv()
+            return dot16(unlower, stack_right(raw), NN)
+
+        return unlower, lefts, finish
+
+    def forward(d):
+        if d:
+            base_copies[d].wait_recv()
         slot = lax.rem(far + lines - d, lines) * 2 + near
         fwd_copies.append(send(base_all.at[slot], base_all.at[slot], fwd_ss.at[d], fwd_rs.at[d], {"rep": partner}))
-    left_two = left_total(1, right_one)
-    left_full, unlower, finish_two = right_total(1, left_two)
-    un_high, un_low = split(unlower)
-    left_high, left_low = split(left_full)
-    ortho = dot16(
-        jnp.concatenate([un_high, un_low, un_high], axis=1),
-        jnp.concatenate([left_high, left_high, left_low], axis=0),
-        NN,
-    )
-    ortho_high, ortho_low = split(ortho)
-    ortho_cat = jnp.concatenate([ortho_high, ortho_low, ortho_high], axis=0)
-    for r in range(reps):
-        ortho_ref[r] = ortho_cat[:, r * rows : (r + 1) * rows].T
-
-    for copy in vec_copies:
+
+    fwd_copies, vec_copies, vtp_copies = [], [], []
+
+    def during_one():
+        send_base(lines - 1)
+        for k in range(1, reps):
+            vec_copies.append(send(vec_all.at[me], vec_all.at[me], vec_ss.at[k], vec_rs.at[k], {"rep": rep_peer(k)}))
+        forward(0)
+        for d in range(1, lines - 2):
+            forward(d)
+
+    def during_two():
+        for copy in vec_copies:
+            copy.wait_recv()
+        vec_sum = vec_all[0]
+        for r in range(1, reps):
+            vec_sum = vec_sum + vec_all[r]
+        vec_tp[col] = vec_sum
+        for k in range(1, tps):
+            vtp_copies.append(send(vec_tp.at[col], vec_tp.at[col], vtp_ss.at[k], vtp_rs.at[k], {"tp": tp_peer(k)}))
+        for d in range(max(1, lines - 2), lines):
+            forward(d)
+
+    left_one = left_total(0, warm_ref[...], during_one)
+    _, _, finish_one = right_total(0, left_one)
+    left_two = left_total(1, finish_one(), during_two)
+    unlower, lefts, finish_two = right_total(1, left_two)
+
+    stores = []
+
+    def store(src, dst):
+        stores.append(pltpu.make_async_copy(src, dst, out_sem.at[len(stores)]))
+        stores[-1].start()
+
+    for copy in vtp_copies:
         copy.wait_recv()
-    vec_sum = vec_all[0]
-    for r in range(1, reps):
-        vec_sum = vec_sum + vec_all[r]
-    vsum_ref[...] = vec_sum
+    for t in range(tps):
+        vsum_ref[:, t * quarter : (t + 1) * quarter] = vec_tp[t]
+    store(vsum_ref, vsum_hbm)
     for copy in fwd_copies:
         copy.wait_recv()
+    store(base_all, base_hbm)
+    for copy in lefts:
+        copy.wait_recv()
     for r in range(reps):
-        base_ref[r] = base_all[r]
-    for copy in sent[: len(sent) - (reps - 1)]:
+        ortho = dot16(unlower, stack_right(left_all[r]), NN)
+        ortho_high, ortho_low = split(ortho)
+        ortho_ref[r] = jnp.concatenate([ortho_high, ortho_low, ortho_high], axis=0).T
+    store(ortho_ref, ortho_hbm)
+    right_ref[...] = stack_right(finish_two() / reps)
+    store(right_ref, right_hbm)
+    for copy in sent:
         copy.wait_send()
-
-    right_high, right_low = split(finish_two() / reps)
-    right_ref[...] = jnp.concatenate([right_high, right_high, right_low], axis=0)
-    for copy in sent[len(sent) - (reps - 1) :]:
-        copy.wait_send()
+    for copy in stores:
+        copy.wait()
 
 
 def finish_kernel(
     reps,
-    comb_ref,
-    ortho_ref,
-    right_ref,
-    base_ref,
-    vsum_ref,
+    grad_hbm,
+    old_feed_hbm,
+    ortho_hbm,
+    right_hbm,
+    base_hbm,
+    vsum_hbm,
     mom_hbm,
     master_hbm,
     vpar_hbm,
@@ -393,6 +453,12 @@
     weight_hbm,
     new_vpar_hbm,
     new_vmom_hbm,
+    grad_ref,
+    old_feed_ref,
+    ortho_ref,
+    right_ref,
+    base_ref,
+    vsum_ref,
     mom_ref,
     master_ref,
     vpar_ref,
@@ -400,34 +466,58 @@
     feed_ref,
     weight_ref,
     load_sem,
+    chunk_sem,
     feed_sem,
     weight_sem,
     out_sem,
 ):
     me = lax.axis_index("rep")
     rows = mom_ref.shape[0]
-    loads = []
-    for i, (src, dst) in enumerate(
-        ((mom_hbm, mom_ref), (master_hbm, master_ref), (vpar_hbm, vpar_ref), (vmom_hbm, vmom_ref))
+    loads, chunks = [], []
+
+    def load(src, dst, sem):
+        copy = pltpu.make_async_copy(src, dst, sem)
+        copy.start()
+        return copy
+
+    loads.append(load(right_hbm, right_ref, load_sem.at[0]))
+    for r in range(reps):
+        at = pl.ds(r * rows, rows)
+        chunks.append(
+            (
+                load(ortho_hbm.at[r], ortho_ref.at[r], chunk_sem.at[0, r]),
+                load(grad_hbm.at[at, :], grad_ref.at[at, :], chunk_sem.at[1, r]),
+                load(old_feed_hbm.at[at, :], old_feed_ref.at[at, :], chunk_sem.at[2, r]),
+                load(base_hbm.at[r], base_ref.at[r], chunk_sem.at[3, r]),
+            )
+        )
+    for src, dst in (
+        (vsum_hbm, vsum_ref),
+        (mom_hbm, mom_ref),
+        (master_hbm, master_ref),
+        (vpar_hbm, vpar_ref),
+        (vmom_hbm, vmom_ref),
     ):
-        loads.append(pltpu.make_async_copy(src, dst, load_sem.at[i]))
-        loads[i].start()
+        loads.append(load(src, dst, load_sem.at[len(loads)]))
     stores = []
 
     def store(src, dst, sem):
         stores.append(pltpu.make_async_copy(src, dst, sem))
         stores[-1].start()
 
+    loads[0].wait()
     right = right_ref[...]
     for r in range(reps):
         at = pl.ds(r * rows, rows)
+        for copy in chunks[r]:
+            copy.wait()
         approx = dot16(ortho_ref[r], right, NN)
-        feed_ref[at, :] = comb_ref[at, :] - approx
+        feed_ref[at, :] = grad_ref[at, :].astype(jnp.float32) + old_feed_ref[at, :] - approx
         store(feed_ref.at[at, :], new_feed_hbm.at[at, :], feed_sem.at[r])
         weight_ref[at, :] = (base_ref[r].astype(jnp.float32) - LEARN_RATE * approx).astype(jnp.bfloat16)
         store(weight_ref.at[at, :], weight_hbm.at[at, :], weight_sem.at[r])
     own = dot16(ortho_ref[me], right, NN)
-    for copy in loads:
+    for copy in loads[1:]:
         copy.wait()
     momentum = MOMENTUM_RATE * mom_ref[...] + own
     mom_ref[...] = momentum
@@ -454,22 +544,24 @@
     lines = reps // 2
     f32, bf16 = jnp.float32, jnp.bfloat16
     dma = pltpu.SemaphoreType.DMA
-    vmem = pl.BlockSpec(memory_space=pltpu.VMEM)
     hbm = pl.BlockSpec(memory_space=pltpu.HBM)
     whole = feedback.shape[1:]
     shape = jax.ShapeDtypeStruct
     parts = pl.pallas_call(
         functools.partial(step_kernel, reps, tps),
         out_shape=(
-            shape(whole, f32),
             shape((reps, rows, 3 * rank), bf16),
             shape((3 * rank, cols), bf16),
             shape((reps, rows, cols), bf16),
             shape((1, vec), f32),
         ),
         in_specs=[hbm] * 6,
-        out_specs=(vmem,) * 5,
+        out_specs=(hbm,) * 4,
         scratch_shapes=[
+            pltpu.VMEM((reps, rows, 3 * rank), bf16),
+            pltpu.VMEM((3 * rank, cols), bf16),
+            pltpu.VMEM((1, vec), f32),
+            dma((4,)),
             pltpu.VMEM(whole, bf16),
             pltpu.VMEM(whole, f32),
             pltpu.VMEM((rank, cols), f32),
@@ -484,23 +576,27 @@
             pltpu.VMEM((reps, rows, cols), bf16),
             pltpu.VMEM((2, rank, rows), f32),
             pltpu.VMEM((2, tps, rank, rows), f32),
-            pltpu.VMEM((2, reps, rank, rows), f32),
+            pltpu.VMEM((reps, rank, rows), f32),
             pltpu.VMEM((2, reps, SUBLANES, LANES), f32),
             pltpu.VMEM((2, reps, SUBLANES, LANES), f32),
             pltpu.VMEM((2, reps, SUBLANES, LANES), f32),
-            pltpu.VMEM((reps, 1, vec), f32),
+            pltpu.VMEM((reps, 1, vec // tps), f32),
+            pltpu.VMEM((tps, 1, vec // tps), f32),
+            pltpu.VMEM((2, reps, SUBLANES, LANES), f32),
             dma((lines,)), dma((lines,)),
             dma((lines,)), dma((lines,)),
             dma((lines,)), dma((lines,)),
             dma((lines,)), dma((lines,)),
             dma((2, tps)), dma((2, tps)),
-            dma((2, reps)), dma((2, reps)),
+            dma((reps,)), dma((reps,)),
             dma((2, reps)), dma((2, reps)),
             dma((2, reps)), dma((2, reps)),
             dma((reps,)), dma((reps,)),
+            dma((tps,)), dma((tps,)),
+            dma((2, reps)), dma((2, reps)),
         ],
         compiler_params=pltpu.CompilerParams(
-            collective_id=0, has_side_effects=True, vmem_limit_bytes=40 * 1024 * 1024
+            collective_id=0, has_side_effects=True, vmem_limit_bytes=56 * 1024 * 1024
         ),
     )(
         gradients[0], feedback[0], warm_factor.T, momentum, master_owned, vector_grads
@@ -515,19 +611,25 @@
             shape((vec,), f32),
             shape((vec,), f32),
         ),
-        in_specs=[vmem] * 5 + [hbm] * 4,
+        in_specs=[hbm] * 10,
         out_specs=(hbm,) * 6,
         scratch_shapes=[
+            pltpu.VMEM(whole, bf16),
+            pltpu.VMEM(whole, f32),
+            pltpu.VMEM((reps, rows, 3 * rank), bf16),
+            pltpu.VMEM((3 * rank, cols), bf16),
+            pltpu.VMEM((reps, rows, cols), bf16),
+            pltpu.VMEM((1, vec), f32),
             pltpu.VMEM((rows, cols), f32),
             pltpu.VMEM((rows, cols), f32),
             pltpu.VMEM((vec,), f32),
             pltpu.VMEM((vec,), f32),
             pltpu.VMEM(whole, f32),
             pltpu.VMEM(whole, bf16),
-            dma((4,)), dma((reps,)), dma((reps,)), dma((4,)),
+            dma((6,)), dma((4, reps)), dma((reps,)), dma((reps,)), dma((4,)),
         ],
-        compiler_params=pltpu.CompilerParams(vmem_limit_bytes=40 * 1024 * 1024),
-    )(*parts, momentum, master_owned, vector_params, vector_momentum)
+        compiler_params=pltpu.CompilerParams(vmem_limit_bytes=56 * 1024 * 1024),
+    )(gradients[0], feedback[0], *parts, momentum, master_owned, vector_params, vector_momentum)
     return (outs[0][None],) + tuple(outs[1:])
 
 
@@ -535,7 +637,8 @@
     rows, cols = arrays[3].shape
     rank = arrays[2].shape[1]
     pieces = (cols // LANES) * (rank // SUBLANES)
-    if reps == pieces and reps % 2 == 0 and rows == LANES:
+    quarter = arrays[5].shape[1] // tps
+    if reps == pieces and reps % 2 == 0 and rows == LANES and quarter % LANES == 0 and rank * SUBLANES * 4 == 8 * LANES:
         return kernel_shards(reps, tps, *arrays)
     return shards(*arrays)
 

time: 53.8 us -> 48.1 us (0.89)
  local copies, waits for them, and re-layouts: 5.54 us -> 0 us
    unnamed x18 -> x0, local copies, waits for them, and re-layouts: 5.54 us -> none
    pallas_call x1, Pallas kernels: 1.96 us -> 4.09 us  [kernel_shards(): pl.pallas_call(functools.partial(finish_kernel, reps), out_shape=(shape(w...]
    pallas_call x1, Pallas kernels: 45.3 us -> 43.2 us  [kernel_shards(): pl.pallas_call(functools.partial(step_kernel, reps, tps), out_shape=(shap...]
where the time goes in v3:
time: 48.1 us; the launch traced here: 48 us
  Pallas kernels  47.3 us (98%)
  between operations  0.64 us (1%)
    pallas_call x1, Pallas kernels, kernel_shards(): pl.pallas_call(functools.partial(step_kernel, reps, tps), out_shape=(shap...  43.2 us
    pallas_call x1, Pallas kernels, kernel_shards(): pl.pallas_call(functools.partial(finish_kernel, reps), out_shape=(shape(w...  4.09 us

profile of v3, /device:TPU:0, one launch (start us, length us, event | category | flops | bytes accessed | tf_op | source)
XLA Modules:
  0.0 48.0 jit_solution(9878227510746179254)
XLA Ops:
  0.6 43.2 %shard_map.127 = (bf16[8,128,96]{2,1,0:T(8,128)(2,1)}, bf16[96,256]{1,0:T(8,128)(2,1)}, bf16[8,128,256]{2,1,0:T(8,128)(2,1)}, f32[1,2560]{1,0:T(1,128)}) custom-call(bf16[1024,256]{1,0:T(8,128)(2,1)} %bitcast.6, f32[1024,256]{1,0:T(8,128)} %bitcast.4, f32[32,256]{1,0:T(8,128)} %bitcast.8, f32[128,256]{1,0:T(8,128)} %mom_hbm.3, f32[128,256]{1,0:T(8,128)} %master_hbm.3, ...), custom_call_target="tpu_custom_call" | custom-call | tf_op jit(solution)/shard_map/pallas_call | solution.py:550
  43.9 4.1 %shard_map.128 = (f32[1024,256]{1,0:T(8,128)}, f32[128,256]{1,0:T(8,128)}, f32[128,256]{1,0:T(8,128)}, bf16[1024,256]{1,0:T(8,128)(2,1)}, f32[2560]{0:T(1024)}, /*index=5*/f32[2560]{0:T(1024)}) custom-call(bf16[1024,256]{1,0:T(8,128)(2,1)} %bitcast.7, f32[1024,256]{1,0:T(8,128)} %bitcast.5, bf16[8,128,96]{2,1,0:T(8,128)(2,1)} %get-tuple-element.16.ortho_hbm, ...), custom_call_target="tpu_custom_call" | custom-call | tf_op jit(solution)/shard_map/pallas_call | solution.py:604

commit v4 on v3

--- a/solution.py
+++ b/solution.py
@@ -180,7 +180,6 @@
     right_all,
     vec_all,
     vec_tp,
-    gram_all,
     pair_ss,
     pair_rs,
     line_ss,
@@ -201,8 +200,6 @@
     vec_rs,
     vtp_ss,
     vtp_rs,
-    gram_ss,
-    gram_rs,
 ):
     me = lax.axis_index("rep")
     col = lax.axis_index("tp")
@@ -278,8 +275,7 @@
             send(base_all.at[me], base_all.at[me], base_ss.at[d], base_rs.at[d], {"rep": line_at(d) * 2 + near})
         )
 
-    for d in range(1, lines - 1):
-        send_base(d)
+    send_base(1)
     line_copies = []
     for d in range(1, lines):
         mine = combined_block(line_at(d) * 2 + near)
@@ -311,33 +307,29 @@
         return part
 
     def right_total(phase, left_t):
-        gram_all[phase, me] = pack_square(gram_of(left_t))
+        packed = pack_square(gram_of(left_t))
         right_t = times_parts(left_t, sum_high, sum_low, NN)
         for s in range(cols // LANES):
             for q in range(half):
-                piece_send[phase, s * half + q] = right_t[
+                piece_send[phase, s * half + q, :SUBLANES] = right_t[
                     q * SUBLANES : (q + 1) * SUBLANES, s * LANES : (s + 1) * LANES
                 ]
-        pieces, grams, rights = [], [], []
+                piece_send[phase, s * half + q, SUBLANES:] = packed
+        pieces, rights = [], []
         for k in range(1, reps):
             pieces.append(
                 send(
-                    piece_send.at[phase, rep_peer(k)], piece_recv.at[phase, k],
+                    piece_send.at[phase, rep_peer(k)], piece_recv.at[phase, me],
                     piece_ss.at[phase, k], piece_rs.at[phase, k], {"rep": rep_peer(k)},
                 )
             )
-        for k in range(1, reps):
-            grams.append(
-                send(
-                    gram_all.at[phase, me], gram_all.at[phase, me],
-                    gram_ss.at[phase, k], gram_rs.at[phase, k], {"rep": rep_peer(k)},
-                )
-            )
-        piece = piece_send[phase, me]
-        for k in range(1, reps):
-            pieces[k - 1].wait_recv()
-            piece = piece + piece_recv[phase, k]
-        right_all[phase, me] = piece
+        piece_recv[phase, me] = piece_send[phase, me]
+        for copy in pieces:
+            copy.wait_recv()
+        both = piece_recv[phase, 0]
+        for r in range(1, reps):
+            both = both + piece_recv[phase, r]
+        right_all[phase, me] = both[:SUBLANES]
         for k in range(1, reps):
             rights.append(
                 send(
@@ -352,12 +344,7 @@
                 lefts.append(
                     send(left_all.at[me], left_all.at[me], left_ss.at[k], left_rs.at[k], {"rep": rep_peer(k)})
                 )
-        for copy in grams:
-            copy.wait_recv()
-        gram = gram_all[phase, 0]
-        for r in range(1, reps):
-            gram = gram + gram_all[phase, r]
-        unlower = stack_left(inverse_lower(unpack_square(gram, rank)))
+        unlower = stack_left(inverse_lower(unpack_square(both[SUBLANES:], rank)))
 
         def finish():
             for copy in rights:
@@ -382,7 +369,8 @@
     fwd_copies, vec_copies, vtp_copies = [], [], []
 
     def during_one():
-        send_base(lines - 1)
+        for d in range(2, lines):
+            send_base(d)
         for k in range(1, reps):
             vec_copies.append(send(vec_all.at[me], vec_all.at[me], vec_ss.at[k], vec_rs.at[k], {"rep": rep_peer(k)}))
         forward(0)
@@ -481,16 +469,17 @@
         return copy
 
     loads.append(load(right_hbm, right_ref, load_sem.at[0]))
-    for r in range(reps):
-        at = pl.ds(r * rows, rows)
+    loads.append(load(ortho_hbm, ortho_ref, load_sem.at[1]))
+    span = reps * rows // 2
+    for h in range(2):
+        at = pl.ds(h * span, span)
         chunks.append(
             (
-                load(ortho_hbm.at[r], ortho_ref.at[r], chunk_sem.at[0, r]),
-                load(grad_hbm.at[at, :], grad_ref.at[at, :], chunk_sem.at[1, r]),
-                load(old_feed_hbm.at[at, :], old_feed_ref.at[at, :], chunk_sem.at[2, r]),
-                load(base_hbm.at[r], base_ref.at[r], chunk_sem.at[3, r]),
+                load(grad_hbm.at[at, :], grad_ref.at[at, :], chunk_sem.at[0, h]),
+                load(old_feed_hbm.at[at, :], old_feed_ref.at[at, :], chunk_sem.at[1, h]),
             )
         )
+    loads.append(load(base_hbm, base_ref, load_sem.at[2]))
     for src, dst in (
         (vsum_hbm, vsum_ref),
         (mom_hbm, mom_ref),
@@ -506,18 +495,25 @@
         stores[-1].start()
 
     loads[0].wait()
+    loads[1].wait()
     right = right_ref[...]
     for r in range(reps):
         at = pl.ds(r * rows, rows)
-        for copy in chunks[r]:
-            copy.wait()
+        if r * rows % span == 0:
+            for copy in chunks[r * rows // span]:
+                copy.wait()
+        if r == 0:
+            loads[2].wait()
         approx = dot16(ortho_ref[r], right, NN)
         feed_ref[at, :] = grad_ref[at, :].astype(jnp.float32) + old_feed_ref[at, :] - approx
-        store(feed_ref.at[at, :], new_feed_hbm.at[at, :], feed_sem.at[r])
         weight_ref[at, :] = (base_ref[r].astype(jnp.float32) - LEARN_RATE * approx).astype(jnp.bfloat16)
-        store(weight_ref.at[at, :], weight_hbm.at[at, :], weight_sem.at[r])
+        if (r + 1) * rows % span == 0:
+            h = r * rows // span
+            out = pl.ds(h * span, span)
+            store(feed_ref.at[out, :], new_feed_hbm.at[out, :], feed_sem.at[h])
+            store(weight_ref.at[out, :], weight_hbm.at[out, :], weight_sem.at[h])
     own = dot16(ortho_ref[me], right, NN)
-    for copy in loads[1:]:
+    for copy in loads[3:]:
         copy.wait()
     momentum = MOMENTUM_RATE * mom_ref[...] + own
     mom_ref[...] = momentum
@@ -577,12 +573,11 @@
             pltpu.VMEM((2, rank, rows), f32),
             pltpu.VMEM((2, tps, rank, rows), f32),
             pltpu.VMEM((reps, rank, rows), f32),
-            pltpu.VMEM((2, reps, SUBLANES, LANES), f32),
-            pltpu.VMEM((2, reps, SUBLANES, LANES), f32),
+            pltpu.VMEM((2, reps, 2 * SUBLANES, LANES), f32),
+            pltpu.VMEM((2, reps, 2 * SUBLANES, LANES), f32),
             pltpu.VMEM((2, reps, SUBLANES, LANES), f32),
             pltpu.VMEM((reps, 1, vec // tps), f32),
             pltpu.VMEM((tps, 1, vec // tps), f32),
-            pltpu.VMEM((2, reps, SUBLANES, LANES), f32),
             dma((lines,)), dma((lines,)),
             dma((lines,)), dma((lines,)),
             dma((lines,)), dma((lines,)),
@@ -593,7 +588,6 @@
             dma((2, reps)), dma((2, reps)),
             dma((reps,)), dma((reps,)),
             dma((tps,)), dma((tps,)),
-            dma((2, reps)), dma((2, reps)),
         ],
         compiler_params=pltpu.CompilerParams(
             collective_id=0, has_side_effects=True, vmem_limit_bytes=56 * 1024 * 1024
@@ -626,7 +620,7 @@
             pltpu.VMEM((vec,), f32),
             pltpu.VMEM(whole, f32),
             pltpu.VMEM(whole, bf16),
-            dma((6,)), dma((4, reps)), dma((reps,)), dma((reps,)), dma((4,)),
+            dma((8,)), dma((2, 2)), dma((2,)), dma((2,)), dma((4,)),
         ],
         compiler_params=pltpu.CompilerParams(vmem_limit_bytes=56 * 1024 * 1024),
     )(gradients[0], feedback[0], *parts, momentum, master_owned, vector_params, vector_momentum)

time: 48.1 us -> 47.4 us (0.985)
  Pallas kernels: 47.3 us -> 46.6 us
    pallas_call x1, Pallas kernels: 4.09 us -> 3.08 us  [kernel_shards(): pl.pallas_call(functools.partial(finish_kernel, reps), out_shape=(shape(w...]
where the time goes in v4:
time: 47.4 us; the launch traced here: 47.2 us
  Pallas kernels  46.6 us (98%)
  between operations  0.64 us (1%)
    pallas_call x1, Pallas kernels, kernel_shards(): pl.pallas_call(functools.partial(step_kernel, reps, tps), out_shape=(shap...  43.5 us
    pallas_call x1, Pallas kernels, kernel_shards(): pl.pallas_call(functools.partial(finish_kernel, reps), out_shape=(shape(w...  3.08 us

profile of v4, /device:TPU:0, one launch (start us, length us, event | category | flops | bytes accessed | tf_op | source)
XLA Modules:
  0.0 47.2 jit_solution(17319042810255013154)
XLA Ops:
  0.6 43.5 %shard_map.127 = (bf16[8,128,96]{2,1,0:T(8,128)(2,1)}, bf16[96,256]{1,0:T(8,128)(2,1)}, bf16[8,128,256]{2,1,0:T(8,128)(2,1)}, f32[1,2560]{1,0:T(1,128)}) custom-call(bf16[1024,256]{1,0:T(8,128)(2,1)} %bitcast.6, f32[1024,256]{1,0:T(8,128)} %bitcast.4, f32[32,256]{1,0:T(8,128)} %bitcast.8, f32[128,256]{1,0:T(8,128)} %mom_hbm.3, f32[128,256]{1,0:T(8,128)} %master_hbm.3, ...), custom_call_target="tpu_custom_call" | custom-call | tf_op jit(solution)/shard_map/pallas_call | solution.py:546
  44.1 3.1 %shard_map.128 = (f32[1024,256]{1,0:T(8,128)}, f32[128,256]{1,0:T(8,128)}, f32[128,256]{1,0:T(8,128)}, bf16[1024,256]{1,0:T(8,128)(2,1)}, f32[2560]{0:T(1024)}, /*index=5*/f32[2560]{0:T(1024)}) custom-call(bf16[1024,256]{1,0:T(8,128)(2,1)} %bitcast.7, f32[1024,256]{1,0:T(8,128)} %bitcast.5, bf16[8,128,96]{2,1,0:T(8,128)(2,1)} %get-tuple-element.16.ortho_hbm, ...), custom_call_target="tpu_custom_call" | custom-call | tf_op jit(solution)/shard_map/pallas_call | solution.py:598

commit v5 on v4

--- a/solution.py
+++ b/solution.py
@@ -261,8 +261,12 @@
     pl.semaphore_wait(barrier, reps - 1 + tps - 1)
 
     pairs = {}
-    for d in order:
+
+    def send_pair(d):
         pairs[d] = send(pair_send.at[d], pair_recv.at[d], pair_ss.at[d], pair_rs.at[d], {"rep": partner})
+
+    for d in order[:2]:
+        send_pair(d)
     for copy in loads[2:]:
         copy.wait()
     base_all[me] = (master_ref[...] - (LEARN_RATE * MOMENTUM_RATE) * mom_ref[...]).astype(jnp.bfloat16)
@@ -275,11 +279,12 @@
             send(base_all.at[me], base_all.at[me], base_ss.at[d], base_rs.at[d], {"rep": line_at(d) * 2 + near})
         )
 
-    send_base(1)
     line_copies = []
     for d in range(1, lines):
         mine = combined_block(line_at(d) * 2 + near)
         pairs[d].wait_recv()
+        if d + 1 < lines:
+            send_pair(order[d + 1])
         line_send[d] = (mine + pair_recv[d].astype(jnp.float32)).astype(jnp.bfloat16)
         line_copies.append(
             send(line_send.at[d], line_recv.at[d], line_ss.at[d], line_rs.at[d], {"rep": line_at(d) * 2 + near})
@@ -366,10 +371,10 @@
         slot = lax.rem(far + lines - d, lines) * 2 + near
         fwd_copies.append(send(base_all.at[slot], base_all.at[slot], fwd_ss.at[d], fwd_rs.at[d], {"rep": partner}))
 
-    fwd_copies, vec_copies, vtp_copies = [], [], []
+    fwd_copies, vec_copies, vtp_copies, early = [], [], [], []
 
     def during_one():
-        for d in range(2, lines):
+        for d in range(1, lines):
             send_base(d)
         for k in range(1, reps):
             vec_copies.append(send(vec_all.at[me], vec_all.at[me], vec_ss.at[k], vec_rs.at[k], {"rep": rep_peer(k)}))
@@ -378,6 +383,10 @@
             forward(d)
 
     def during_two():
+        for copy in sent:
+            if not any(copy is other for other in base_copies + fwd_copies):
+                copy.wait_send()
+                early.append(copy)
         for copy in vec_copies:
             copy.wait_recv()
         vec_sum = vec_all[0]
@@ -418,7 +427,8 @@
     right_ref[...] = stack_right(finish_two() / reps)
     store(right_ref, right_hbm)
     for copy in sent:
-        copy.wait_send()
+        if not any(copy is other for other in early):
+            copy.wait_send()
     for copy in stores:
         copy.wait()
 

time: 47.4 us -> 51.1 us (1.078)
  Pallas kernels: 46.6 us -> 50.3 us
    pallas_call x1, Pallas kernels: 43.5 us -> 47.2 us  [kernel_shards(): pl.pallas_call(functools.partial(step_kernel, reps, tps), out_shape=(shap...]
where the time goes in v5:
time: 51.1 us; the launch traced here: 50.9 us
  Pallas kernels  50.3 us (98%)
  between operations  0.64 us (1%)
    pallas_call x1, Pallas kernels, kernel_shards(): pl.pallas_call(functools.partial(step_kernel, reps, tps), out_shape=(shap...  47.2 us
    pallas_call x1, Pallas kernels, kernel_shards(): pl.pallas_call(functools.partial(finish_kernel, reps), out_shape=(shape(w...  3.08 us

profile of v5, /device:TPU:0, one launch (start us, length us, event | category | flops | bytes accessed | tf_op | source)
XLA Modules:
  0.0 50.9 jit_solution(13599491949819411097)
XLA Ops:
  0.6 47.2 %shard_map.127 = (bf16[8,128,96]{2,1,0:T(8,128)(2,1)}, bf16[96,256]{1,0:T(8,128)(2,1)}, bf16[8,128,256]{2,1,0:T(8,128)(2,1)}, f32[1,2560]{1,0:T(1,128)}) custom-call(bf16[1024,256]{1,0:T(8,128)(2,1)} %bitcast.6, f32[1024,256]{1,0:T(8,128)} %bitcast.4, f32[32,256]{1,0:T(8,128)} %bitcast.8, f32[128,256]{1,0:T(8,128)} %mom_hbm.3, f32[128,256]{1,0:T(8,128)} %master_hbm.3, ...), custom_call_target="tpu_custom_call" | custom-call | tf_op jit(solution)/shard_map/pallas_call | solution.py:556
  47.8 3.1 %shard_map.128 = (f32[1024,256]{1,0:T(8,128)}, f32[128,256]{1,0:T(8,128)}, f32[128,256]{1,0:T(8,128)}, bf16[1024,256]{1,0:T(8,128)(2,1)}, f32[2560]{0:T(1024)}, /*index=5*/f32[2560]{0:T(1024)}) custom-call(bf16[1024,256]{1,0:T(8,128)(2,1)} %bitcast.7, f32[1024,256]{1,0:T(8,128)} %bitcast.5, bf16[8,128,96]{2,1,0:T(8,128)(2,1)} %get-tuple-element.16.ortho_hbm, ...), custom_call_target="tpu_custom_call" | custom-call | tf_op jit(solution)/shard_map/pallas_call | solution.py:608
